TPU v7x, 1024 devices: a whole 4x4x32 slice. The times are simulated.
1024 devices in a mesh: wide: 64 (over z, core), narrow: 16 (over y, x).
Axes of the slice: x: 4, y: 4, z: 32, core: 2. Of those that a mesh axis runs over, the one named last changes fastest.
Arguments:
- grad: bfloat16 [64, 1792, 1024], P('wide', 'narrow'), may hold values from -60 to 60, as said below
- momentum: bfloat16 [64, 2, 1792, 1024], P('wide', None, 'narrow'), may hold values from -6 to 6
- owner: int32 [32], replicated, may hold values from 0 to 63, as said below
Outputs:
- update: bfloat16 [64, 1792, 1024], P('wide', 'narrow')
- new_momentum: bfloat16 [64, 2, 1792, 1024], P('wide', None, 'narrow')
Inputs may be any that keep to these rules, and one draw needn't show every extreme that they name: `grad`: finite values. owner[e] is 2e-1, 2e, 2e+1 or 2e+2, taken modulo 2 * 32; no two experts have the same owner.
All inputs are finite; a program needn't handle non-finite values.
Results may differ from a plain program's by a relative error of at most 0.02.
Values may be sent and summed in bfloat16 or wider, within the bound.
A program may use at most 32 MiB of HBM per device.

v0:
```python
import jax
import jax.numpy as jnp
from jax import lax
from jax.sharding import PartitionSpec as P

D = 3584


momentum_rate = 0.9
norm_eps = 1e-07


def shifted(value, axis, steps):
    count = lax.axis_size(axis)
    pairs = [(source, (source + steps) % count) for source in range(count)]
    return lax.ppermute(value, axis, pairs)


def orthogonalize(block):
    width = block.shape[1]
    columns = block
    gram_rows = lax.psum_scatter(
        lax.dot_general(
            columns, block, (((0,), (0,)), ((), ())), preferred_element_type=jnp.float32
        ).astype(jnp.bfloat16),
        "narrow",
        scatter_dimension=0,
        tiled=True,
    )
    piece = lax.all_gather(gram_rows, "narrow", axis=0, tiled=True)
    columns = block
    product = jnp.dot(columns, piece, preferred_element_type=jnp.float32)
    row_ids = lax.broadcasted_iota(jnp.int32, piece.shape, 0)
    col_ids = lax.broadcasted_iota(jnp.int32, piece.shape, 1)
    trace_sum = jnp.sum(jnp.where(row_ids == col_ids, piece.astype(jnp.float32), 0.0))
    product, trace_sum = (product, trace_sum)
    factor = jnp.sqrt(jnp.float32(width)) / (jnp.sqrt(trace_sum) + norm_eps)
    result = factor * (1.5 * block.astype(jnp.float32) - 0.5 * factor * factor * product)
    return result * jnp.sqrt(jnp.float32(D))


def expert_step(halves, stored):
    grad_value = halves.astype(jnp.float32)
    velocity = momentum_rate * stored.astype(jnp.float32) + grad_value
    block = (grad_value + momentum_rate * velocity).astype(jnp.bfloat16)
    rows = halves.shape[1]
    result = orthogonalize(block.reshape(2 * rows, halves.shape[2]))
    return (velocity, result.reshape(halves.shape))


def body(grad, momentum, owner):
    groups = lax.axis_size("wide")
    experts = groups // 2
    index = lax.axis_index("wide")
    even = index % 2 == 0
    uneven = jnp.logical_not(even)
    middle = index // 2
    other_expert = jnp.where(even, middle - 1, middle + 1) % experts
    owner_main = lax.dynamic_index_in_dim(owner, middle, 0, keepdims=False)
    owner_other = lax.dynamic_index_in_dim(owner, other_expert, 0, keepdims=False)
    live_main = owner_main == index
    live_other = owner_other == index
    local = grad[0]
    fetched = {}
    for offset in (2, 1, -1, -2):
        fetched[offset] = shifted(grad, "wide", offset)[0]
    lower = jnp.where(
        even, jnp.where(live_main, local, fetched[2]), jnp.where(live_main, fetched[1], fetched[-1])
    )
    upper = jnp.where(
        even,
        jnp.where(live_main, fetched[-1], fetched[1]),
        jnp.where(live_main, local, fetched[-2]),
    )
    state, result = expert_step(jnp.stack([lower, upper]), momentum[0])
    live = jnp.logical_or(live_main, live_other)
    new_momentum = jnp.where(live, state, 0.0).astype(jnp.bfloat16)[None]
    part = jnp.where(live, result, 0.0).astype(jnp.bfloat16)
    blank = jnp.zeros_like(part[0])
    even_main = jnp.logical_and(even, live_main)
    even_other = jnp.logical_and(even, live_other)
    odd_main = jnp.logical_and(uneven, live_main)
    odd_other = jnp.logical_and(uneven, live_other)
    outgoing = {
        1: jnp.where(even_main, part[1], jnp.where(odd_other, part[0], blank)),
        -1: jnp.where(even_other, part[1], jnp.where(odd_main, part[0], blank)),
        -2: jnp.where(even_other, part[0], blank),
        2: jnp.where(odd_other, part[1], blank),
    }
    total = jnp.where(live_main, jnp.where(even, part[0], part[1]), blank).astype(jnp.float32)
    for offset in (1, -1, -2, 2):
        arrived = shifted(outgoing[offset], "wide", offset)
        total = total + arrived.astype(jnp.float32)
    update = total.astype(jnp.bfloat16)[None]
    return (update, new_momentum)


def solution(mesh):
    return jax.shard_map(
        body,
        mesh=mesh,
        in_specs=(P("wide", "narrow", None), P("wide", None, "narrow", None), P()),
        out_specs=(P("wide", "narrow", None), P("wide", None, "narrow", None)),
        check_vma=False,
    )
```

profile of v0, /device:TPU:1, one launch (start us, length us, event | category | flops | bytes accessed | tf_op | source)
XLA Modules:
  0.0 258.6 jit_solution(7677648644647412590)
XLA Ops:
  7.2 0.0 reduce-scatter.2.cloned.1.call-start
  7.2 3.0 %collective-permute-start.1 = (bf16[1,112,1024]{2,1,0:T(8,128)(2,1)}, bf16[1,112,1024]{2,1,0:T(8,128)(2,1)S(1)}, u32[]{:S(2)}, u32[]{:S(2)}) collective-permute-start(bf16[1,112,1024]{2,1,0:T(8,128)(2,1)} %param.3), channel_id=1, source_target_pairs={{0,16},{16,32},{32,48},{48,64},{64,80},{80,96},{96,112},{112,128},... | collective-permute-start | bytes 688136 | tf_op jit(solution)/shard_map/ppermute | solution.py:16
  10.2 3.5 %collective-permute-start = (bf16[1,112,1024]{2,1,0:T(8,128)(2,1)}, bf16[1,112,1024]{2,1,0:T(8,128)(2,1)S(1)}, u32[]{:S(2)}, u32[]{:S(2)}) collective-permute-start(bf16[1,112,1024]{2,1,0:T(8,128)(2,1)} %param.3), channel_id=1, source_target_pairs={{0,32},{16,48},{32,64},{48,80},{64,96},{80,112},{96,128},{112,144}... | collective-permute-start | bytes 688136 | tf_op jit(solution)/shard_map/ppermute | solution.py:16
  13.8 9.5 %collective-permute-start.2 = (bf16[1,112,1024]{2,1,0:T(8,128)(2,1)}, bf16[1,112,1024]{2,1,0:T(8,128)(2,1)S(1)}, u32[]{:S(2)}, u32[]{:S(2)}) collective-permute-start(bf16[1,112,1024]{2,1,0:T(8,128)(2,1)} %param.3), channel_id=1, source_target_pairs={{0,1008},{16,0},{32,16},{48,32},{64,48},{80,64},{96,80},{112,96},{... | collective-permute-start | bytes 688136 | tf_op jit(solution)/shard_map/ppermute | solution.py:16
  23.3 5.7 %collective-permute-start.3 = (bf16[1,112,1024]{2,1,0:T(8,128)(2,1)}, bf16[1,112,1024]{2,1,0:T(8,128)(2,1)S(1)}, u32[]{:S(2)}, u32[]{:S(2)}) collective-permute-start(bf16[1,112,1024]{2,1,0:T(8,128)(2,1)} %param.3), channel_id=1, source_target_pairs={{0,992},{16,1008},{32,0},{48,16},{64,32},{80,48},{96,64},{112,80},... | collective-permute-start | bytes 688136 | tf_op jit(solution)/shard_map/ppermute | solution.py:16
  29.1 1.3 fusion.14
  31.1 0.0 collective-permute-done.1
  31.1 1.9 collective-permute-done
  33.0 0.0 collective-permute-done.2
  33.0 0.5 collective-permute-done.3
  33.5 1.0 select_select_fusion.3
  34.5 3.5 %bitcast_convert_fusion = bf16[1024,1024]{1,0:T(8,128)(2,1)} fusion(bf16[1,2,112,1024]{3,2,1,0:T(8,128)(2,1)} %param.4, bf16[1,1,112,1024]{3,2,1,0:T(8,128)(2,1)S(1)} %bitcast.20, bf16[1,1,112,1024]{3,2,1,0:T(8,128)(2,1)S(1)} %bitcast.18), kind=kOutput, calls=%fused_computation | convolution fusion | flops 472645632 | bytes 3014656 | tf_op jit(solution)/shard_map/dot_general | solution.py:23
  38.0 0.0 copy-start.1
  38.0 0.0 reduce-scatter.2.cloned.1.call-update
  38.0 0.0 all-gather.2.cloned.1.call-start
  38.1 105.9 %reduce-scatter.2.cloned.1.call-done = bf16[64,1024]{1,0:T(8,128)(2,1)} async-done(((bf16[1024,1024]{1,0:T(8,128)(2,1)}), bf16[64,1024]{1,0:T(8,128)(2,1)}) %reduce-scatter.2.cloned.1.call-update) | async-done | bytes 131088 | tf_op jit(solution)/shard_map/reduce_scatter | solution.py:22
  144.0 0.0 all-gather.2.cloned.1.call-update
  144.7 0.0 copy-done.1
  144.8 1.0 select_convert_fusion
  145.7 0.2 fusion.7
  145.9 84.2 %all-gather.2.cloned.1.call-done = bf16[1024,1024]{1,0:T(8,128)(2,1)} async-done(((bf16[64,1024]{1,0:T(8,128)(2,1)}), bf16[1024,1024]{1,0:T(8,128)(2,1)}) %all-gather.2.cloned.1.call-update) | async-done | bytes 2097168 | tf_op jit(solution)/shard_map/all_gather | solution.py:30
  230.1 0.0 copy-start
  230.1 2.5 select_reduce_fusion
  233.4 0.0 copy-done
  233.4 0.8 fusion.4
  234.1 0.1 select_select_fusion.1
  234.2 2.7 %collective-permute-start.4 = (bf16[112,1024]{1,0:T(8,128)(2,1)S(1)}, bf16[112,1024]{1,0:T(8,128)(2,1)S(1)}, u32[]{:S(2)}, u32[]{:S(2)}) collective-permute-start(bf16[112,1024]{1,0:T(8,128)(2,1)S(1)} %get-tuple-element.6), channel_id=1, source_target_pairs={{0,16},{16,32},{32,48},{48,64},{64,80},{80,96},{96,112},{112,128},... | collective-permute-start | bytes 688136 | tf_op jit(solution)/shard_map/ppermute | solution.py:16
  236.9 0.0 collective-permute-start.5
  236.9 6.0 %collective-permute-start.6 = (bf16[112,1024]{1,0:T(8,128)(2,1)S(1)}, bf16[112,1024]{1,0:T(8,128)(2,1)S(1)}, u32[]{:S(2)}, u32[]{:S(2)}) collective-permute-start(bf16[112,1024]{1,0:T(8,128)(2,1)S(1)} %get-tuple-element.8), channel_id=1, source_target_pairs={{0,992},{16,1008},{32,0},{48,16},{64,32},{80,48},{96,64},{112,80},... | collective-permute-start | bytes 688136 | tf_op jit(solution)/shard_map/ppermute | solution.py:16
  242.9 1.9 collective-permute-start.7
  244.8 0.0 collective-permute-done.4
  244.8 0.0 collective-permute-done.5
  244.8 1.0 collective-permute-done.6
  245.8 5.0 %collective-permute-done.7 = bf16[112,1024]{1,0:T(8,128)(2,1)S(1)} collective-permute-done((bf16[112,1024]{1,0:T(8,128)(2,1)S(1)}, bf16[112,1024]{1,0:T(8,128)(2,1)S(1)}, u32[]{:S(2)}, u32[]{:S(2)}) %collective-permute-start.7) | collective-permute-done | bytes 229408 | tf_op jit(solution)/shard_map/ppermute | solution.py:16
  250.9 0.9 fusion.11
  (1 shorter events, 0.0 us)
Async XLA Ops:
  7.2 136.8 %reduce-scatter.2.cloned.1.call-start = ((), (), s32[]{:S(2)}) async-start(), calls=%async_computation.1 | async-start | bytes 2228224 | tf_op jit(solution)/shard_map/reduce_scatter | solution.py:22
  7.2 23.9 %collective-permute-start.1 = (bf16[1,112,1024]{2,1,0:T(8,128)(2,1)}, bf16[1,112,1024]{2,1,0:T(8,128)(2,1)S(1)}, u32[]{:S(2)}, u32[]{:S(2)}) collective-permute-start(bf16[1,112,1024]{2,1,0:T(8,128)(2,1)} %param.3), channel_id=1, source_target_pairs={{0,16},{16,32},{32,48},{48,64},{64,80},{80,96},{96,112},{112,128},... | collective-permute-start | bytes 688136 | tf_op jit(solution)/shard_map/ppermute | solution.py:16
  10.2 22.7 %collective-permute-start = (bf16[1,112,1024]{2,1,0:T(8,128)(2,1)}, bf16[1,112,1024]{2,1,0:T(8,128)(2,1)S(1)}, u32[]{:S(2)}, u32[]{:S(2)}) collective-permute-start(bf16[1,112,1024]{2,1,0:T(8,128)(2,1)} %param.3), channel_id=1, source_target_pairs={{0,32},{16,48},{32,64},{48,80},{64,96},{80,112},{96,128},{112,144}... | collective-permute-start | bytes 688136 | tf_op jit(solution)/shard_map/ppermute | solution.py:16
  13.8 19.2 %collective-permute-start.2 = (bf16[1,112,1024]{2,1,0:T(8,128)(2,1)}, bf16[1,112,1024]{2,1,0:T(8,128)(2,1)S(1)}, u32[]{:S(2)}, u32[]{:S(2)}) collective-permute-start(bf16[1,112,1024]{2,1,0:T(8,128)(2,1)} %param.3), channel_id=1, source_target_pairs={{0,1008},{16,0},{32,16},{48,32},{64,48},{80,64},{96,80},{112,96},{... | collective-permute-start | bytes 688136 | tf_op jit(solution)/shard_map/ppermute | solution.py:16
  23.3 10.2 %collective-permute-start.3 = (bf16[1,112,1024]{2,1,0:T(8,128)(2,1)}, bf16[1,112,1024]{2,1,0:T(8,128)(2,1)S(1)}, u32[]{:S(2)}, u32[]{:S(2)}) collective-permute-start(bf16[1,112,1024]{2,1,0:T(8,128)(2,1)} %param.3), channel_id=1, source_target_pairs={{0,992},{16,1008},{32,0},{48,16},{64,32},{80,48},{96,64},{112,80},... | collective-permute-start | bytes 688136 | tf_op jit(solution)/shard_map/ppermute | solution.py:16
  38.0 106.7 %copy-start.1 = (bf16[1,2,112,1024]{3,2,1,0:T(8,128)(2,1)S(1)}, bf16[1,2,112,1024]{3,2,1,0:T(8,128)(2,1)}, u32[]{:S(2)}) copy-start(bf16[1,2,112,1024]{3,2,1,0:T(8,128)(2,1)} %param.4) | copy-start | bytes 1376260
  38.0 192.1 %all-gather.2.cloned.1.call-start = ((), (), s32[]{:S(2)}) async-start(), calls=%async_computation.2 | async-start | bytes 2228224 | tf_op jit(solution)/shard_map/all_gather | solution.py:30
  230.1 3.2 %copy-start = (bf16[1024,1024]{1,0:T(8,128)(2,1)S(1)}, bf16[1024,1024]{1,0:T(8,128)(2,1)}, u32[]{:S(2)}) copy-start(bf16[1024,1024]{1,0:T(8,128)(2,1)} %all-gather.2.cloned.1.call-done) | copy-start | bytes 6291460
  234.2 10.6 %collective-permute-start.4 = (bf16[112,1024]{1,0:T(8,128)(2,1)S(1)}, bf16[112,1024]{1,0:T(8,128)(2,1)S(1)}, u32[]{:S(2)}, u32[]{:S(2)}) collective-permute-start(bf16[112,1024]{1,0:T(8,128)(2,1)S(1)} %get-tuple-element.6), channel_id=1, source_target_pairs={{0,16},{16,32},{32,48},{48,64},{64,80},{80,96},{96,112},{112,128},... | collective-permute-start | bytes 688136 | tf_op jit(solution)/shard_map/ppermute | solution.py:16
  236.9 7.9 %collective-permute-start.5 = (bf16[112,1024]{1,0:T(8,128)(2,1)S(1)}, bf16[112,1024]{1,0:T(8,128)(2,1)S(1)}, u32[]{:S(2)}, u32[]{:S(2)}) collective-permute-start(bf16[112,1024]{1,0:T(8,128)(2,1)S(1)} %get-tuple-element.7), channel_id=1, source_target_pairs={{0,1008},{16,0},{32,16},{48,32},{64,48},{80,64},{96,80},{112,96},{... | collective-permute-start | bytes 688136 | tf_op jit(solution)/shard_map/ppermute | solution.py:16
  236.9 8.9 %collective-permute-start.6 = (bf16[112,1024]{1,0:T(8,128)(2,1)S(1)}, bf16[112,1024]{1,0:T(8,128)(2,1)S(1)}, u32[]{:S(2)}, u32[]{:S(2)}) collective-permute-start(bf16[112,1024]{1,0:T(8,128)(2,1)S(1)} %get-tuple-element.8), channel_id=1, source_target_pairs={{0,992},{16,1008},{32,0},{48,16},{64,32},{80,48},{96,64},{112,80},... | collective-permute-start | bytes 688136 | tf_op jit(solution)/shard_map/ppermute | solution.py:16
  242.9 8.0 %collective-permute-start.7 = (bf16[112,1024]{1,0:T(8,128)(2,1)S(1)}, bf16[112,1024]{1,0:T(8,128)(2,1)S(1)}, u32[]{:S(2)}, u32[]{:S(2)}) collective-permute-start(bf16[112,1024]{1,0:T(8,128)(2,1)S(1)} %get-tuple-element.9), channel_id=1, source_target_pairs={{0,32},{16,48},{32,64},{48,80},{64,96},{80,112},{96,128},{112,144}... | collective-permute-start | bytes 688136 | tf_op jit(solution)/shard_map/ppermute | solution.py:16
Sparse Core Ops, SparseCore 0:
  38.1 105.8 reduce-scatter.1
  148.9 81.1 all-gather.1
where the time goes:
time: 260 us; the launch traced here: 259 us
  waiting for transfers between devices  199 us (77%)
  starting transfers between devices  32.5 us (12%)
  between operations  16.3 us (6%)
  other arithmetic  5.67 us (2%)
  matrix products  4.25 us (2%)
    reduce_scatter x1, waiting for transfers between devices, orthogonalize(): lax.psum_scatter(lax.dot_general(columns, block, (((0,), (0,)), ((), ()))...  106 us
    all_gather x1, waiting for transfers between devices, orthogonalize(): piece = lax.all_gather(gram_rows, 'narrow', axis=0, tiled=True)  84.2 us
    ppermute x8, starting transfers between devices, shifted(): return lax.ppermute(value, axis, pairs)  32.4 us
    ppermute x8, waiting for transfers between devices, shifted(): return lax.ppermute(value, axis, pairs)  8.41 us
  transfers between devices with their start and end apart: 10, of which 6 were waited for; matrix products, arithmetic and copies ran while one was open for 1% of the time, Pallas kernels for 0%

commit v1 on v0

v1 whole, which is shorter than its diff:
```python
import functools

import jax
import jax.numpy as jnp
from jax import lax
from jax.experimental import pallas as pl
from jax.experimental.pallas import tpu as pltpu
from jax.sharding import PartitionSpec as P

D = 3584
SIDE = 4
TILE = 256

momentum_rate = 0.9
norm_eps = 1e-07

TILES = (
    ((0, 0), (1, 1), (0, 1), (0, 2), (1, 3)),
    ((2, 2), (3, 3), (2, 3), (0, 3), (1, 2)),
)


def kernel(
    planes,
    owner_ref,
    grad_ref,
    mom_ref,
    upd_ref,
    newm_ref,
    g_own,
    g_nb,
    m_loc,
    m_in,
    xf,
    part,
    r1,
    s1,
    r2,
    gram,
    local_sem,
    m_send,
    m_recv,
    g_send,
    g_recv,
    x_send,
    x_recv,
    a_send,
    a_recv,
    b_send,
    b_recv,
    c_send,
    c_recv,
    d_send,
    d_recv,
    e_send,
    e_recv,
):
    rows = grad_ref.shape[1]
    w = lax.axis_index("wide")
    n = lax.axis_index("narrow")
    z, c = w // 2, w % 2
    y, x = n // SIDE, n % SIDE
    up, down = (z + 1) % planes, (z + planes - 1) % planes
    sibling = (z * 2 + 1 - c, n)
    near = jnp.where(c == 0, down, up)

    first = jnp.where(c == 0, x, y)
    second = jnp.where(c == 0, y, x)

    def first_peer(k):
        there = (first + k) % SIDE
        return (w, jnp.where(c == 0, y * SIDE + there, there * SIDE + x))

    def second_peer(k):
        there = (second + k) % SIDE
        return (w, jnp.where(c == 0, there * SIDE + x, y * SIDE + there))

    def remote(src, dst, send, recv, device):
        return pltpu.make_async_remote_copy(
            src_ref=src,
            dst_ref=dst,
            send_sem=send,
            recv_sem=recv,
            device_id=device,
            device_id_type=pl.DeviceIdType.MESH,
        )

    load_m = pltpu.make_async_copy(mom_ref.at[0], m_loc, local_sem.at[0])
    load_g = pltpu.make_async_copy(grad_ref.at[0], g_own.at[c], local_sem.at[1])
    load_m.start()
    load_g.start()

    barrier = pltpu.get_barrier_semaphore()
    partners = [sibling, (near * 2, n), (near * 2 + 1, n), (jnp.where(c == 0, up, down) * 2 + c, n)]
    for k in range(1, SIDE):
        partners += [first_peer(k), second_peer(k)]
    for device in partners:
        pl.semaphore_signal(barrier, inc=1, device_id=device, device_id_type=pl.DeviceIdType.MESH)
    pl.semaphore_wait(barrier, len(partners))

    slot = jnp.where(c == 0, 2, 1)
    m_copies = [
        remote(mom_ref.at[0, 1 - c], m_in.at[0], m_send.at[0], m_recv.at[0], sibling),
        remote(mom_ref.at[0, 0], m_in.at[slot], m_send.at[1], m_recv.at[slot], (near * 2, n)),
        remote(mom_ref.at[0, 1], m_in.at[slot], m_send.at[2], m_recv.at[slot], (near * 2 + 1, n)),
    ]
    for copy in m_copies:
        copy.start()
    load_m.wait()
    load_g.wait()
    for k in range(3):
        remote(m_in.at[k], m_in.at[k], m_send.at[k], m_recv.at[k], sibling).wait_recv()

    offset = (owner_ref[z] - 2 * z + 2 * planes) % (2 * planes)
    mine = pl.ds(pl.multiple_of(c * rows, 16), rows)
    stored = jnp.where(
        offset == c,
        m_loc[c],
        jnp.where(offset == 1 - c, m_in[0], jnp.where(offset == 2, m_in[2], m_in[1])),
    )
    grad_value = g_own[c].astype(jnp.float32)
    velocity = momentum_rate * stored.astype(jnp.float32) + grad_value
    xf[mine, :] = (grad_value + momentum_rate * velocity).astype(jnp.bfloat16)
    x_copy = remote(xf.at[mine], xf.at[mine], x_send, x_recv, sibling)
    x_copy.start()

    g_copies = [
        remote(grad_ref.at[0], g_own.at[c], g_send.at[0], g_recv.at[0], sibling),
        remote(grad_ref.at[0], g_nb.at[c], g_send.at[1], g_recv.at[1 + c], (up * 2, n)),
        remote(grad_ref.at[0], g_nb.at[c], g_send.at[2], g_recv.at[1 + c], (down * 2 + 1, n)),
    ]
    for copy in g_copies:
        copy.start()
    x_copy.wait()

    for t in range(5):
        i = jnp.where(c == 0, TILES[0][t][0], TILES[1][t][0])
        j = jnp.where(c == 0, TILES[0][t][1], TILES[1][t][1])
        left = xf[:, pl.ds(pl.multiple_of(i * TILE, TILE), TILE)]
        right = xf[:, pl.ds(pl.multiple_of(j * TILE, TILE), TILE)]
        tile = lax.dot_general(left, right, (((0,), (0,)), ((), ())), preferred_element_type=jnp.float32)
        part[t * TILE : (t + 1) * TILE, :] = tile.astype(jnp.bfloat16)

    total = part.shape[0]
    quarter = total // SIDE
    piece = quarter // SIDE

    def quarter_at(k):
        return pl.ds(pl.multiple_of(k * quarter, 16), quarter)

    def piece_at(k):
        return pl.ds(pl.multiple_of(k * piece, 16), piece)

    a_copies = []
    for k in (2, 1, 3):
        there = (first + k) % SIDE
        copy = remote(part.at[quarter_at(there)], r1.at[k - 1], a_send.at[k - 1], a_recv.at[k - 1], first_peer(k))
        copy.start()
        a_copies.append(copy)
    acc = part[quarter_at(first), :].astype(jnp.float32)
    for copy in a_copies:
        copy.wait_recv()
    for k in range(3):
        acc = acc + r1[k].astype(jnp.float32)
    s1[...] = acc.astype(jnp.bfloat16)

    b_copies = []
    for k in (2, 1, 3):
        there = (second + k) % SIDE
        copy = remote(s1.at[piece_at(there)], r2.at[k - 1], b_send.at[k - 1], b_recv.at[k - 1], second_peer(k))
        copy.start()
        b_copies.append(copy)
    acc = s1[piece_at(second), :].astype(jnp.float32)
    for copy in b_copies:
        copy.wait_recv()
    for k in range(3):
        acc = acc + r2[k].astype(jnp.float32)

    own = pl.ds(pl.multiple_of(first * quarter + second * piece, 16), piece)
    gram[c, own, :] = acc.astype(jnp.bfloat16)
    c_copies = []
    for k in (2, 1, 3):
        copy = remote(gram.at[c, own], gram.at[c, own], c_send.at[k - 1], c_recv.at[k - 1], second_peer(k))
        copy.start()
        c_copies.append(copy)

    for copy in g_copies:
        copy.wait_send()
    for k in range(3):
        remote(g_own.at[0], g_own.at[0], g_send.at[k], g_recv.at[k], sibling).wait_recv()
    live_main = owner_ref[z] == w
    live_near = owner_ref[near] == w
    for h in range(2):
        arrived = jnp.where(live_main, g_own[h], g_nb[h]).astype(jnp.float32)
        state = momentum_rate * m_loc[h].astype(jnp.float32) + arrived
        newm_ref[0, h] = jnp.where(jnp.logical_or(live_main, live_near), state, 0.0).astype(jnp.bfloat16)

    for copy in c_copies:
        copy.wait_recv()
    d_copies = []
    for k in (2, 1, 3):
        here = quarter_at(first)
        copy = remote(gram.at[c, here], gram.at[c, here], d_send.at[k - 1], d_recv.at[k - 1], first_peer(k))
        copy.start()
        d_copies.append(copy)

    e_copies = []
    for k in (0, 1, 3, 2):
        here = quarter_at((first + SIDE - k) % SIDE)
        if k:
            remote(gram.at[c, here], gram.at[c, here], d_send.at[k - 1], d_recv.at[k - 1], sibling).wait_recv()
        copy = remote(gram.at[c, here], gram.at[c, here], e_send.at[k], e_recv.at[k], sibling)
        copy.start()
        e_copies.append(copy)
    for copy in e_copies:
        copy.wait_recv()

    row_ids = lax.broadcasted_iota(jnp.int32, (TILE, TILE), 0)
    col_ids = lax.broadcasted_iota(jnp.int32, (TILE, TILE), 1)
    diagonal = jnp.zeros((TILE, TILE), jnp.float32)
    place = {}
    for core in range(2):
        for t, pair in enumerate(TILES[core]):
            place[pair] = (core, t)
            if pair[0] == pair[1]:
                tile = gram[core, t * TILE : (t + 1) * TILE, :].astype(jnp.float32)
                diagonal = diagonal + jnp.where(row_ids == col_ids, tile, 0.0)
    trace_sum = jnp.sum(jnp.sum(diagonal, axis=0, keepdims=True), axis=1, keepdims=True)
    width = grad_ref.shape[2]
    factor = jnp.sqrt(jnp.float32(width)) / (jnp.sqrt(trace_sum) + norm_eps)
    tiles = width // TILE
    for j in range(tiles):
        product = jnp.zeros((rows, TILE), jnp.float32)
        for i in range(tiles):
            core, t = place[(min(i, j), max(i, j))]
            tile = gram[core, t * TILE : (t + 1) * TILE, :]
            dims = (((1,), (0,)), ((), ())) if i <= j else (((1,), (1,)), ((), ()))
            product = product + lax.dot_general(
                xf[mine, i * TILE : (i + 1) * TILE], tile, dims, preferred_element_type=jnp.float32
            )
        block = xf[mine, j * TILE : (j + 1) * TILE].astype(jnp.float32)
        result = factor * (1.5 * block - 0.5 * factor * factor * product)
        upd_ref[0, :, j * TILE : (j + 1) * TILE] = (result * jnp.sqrt(jnp.float32(D))).astype(jnp.bfloat16)

    for copy in m_copies + a_copies + b_copies + c_copies + d_copies + e_copies:
        copy.wait_send()


def solution(mesh):
    planes = mesh.shape["wide"] // 2

    def body(grad, momentum, owner):
        rows, width = grad.shape[1:]
        tall = 5 * TILE
        kind = jnp.bfloat16
        dma = pltpu.SemaphoreType.DMA
        return pl.pallas_call(
            functools.partial(kernel, planes),
            out_shape=(
                jax.ShapeDtypeStruct(grad.shape, kind),
                jax.ShapeDtypeStruct(momentum.shape, kind),
            ),
            in_specs=[
                pl.BlockSpec(memory_space=pltpu.SMEM),
                pl.BlockSpec(memory_space=pl.ANY),
                pl.BlockSpec(memory_space=pl.ANY),
            ],
            out_specs=(
                pl.BlockSpec(memory_space=pltpu.VMEM),
                pl.BlockSpec(memory_space=pltpu.VMEM),
            ),
            scratch_shapes=[
                pltpu.VMEM((2, rows, width), kind),
                pltpu.VMEM((2, rows, width), kind),
                pltpu.VMEM((2, rows, width), kind),
                pltpu.VMEM((3, rows, width), kind),
                pltpu.VMEM((2 * rows, width), kind),
                pltpu.VMEM((tall, TILE), kind),
                pltpu.VMEM((3, tall // SIDE, TILE), kind),
                pltpu.VMEM((tall // SIDE, TILE), kind),
                pltpu.VMEM((3, tall // SIDE // SIDE, TILE), kind),
                pltpu.VMEM((2, tall, TILE), kind),
                dma((2,)),
                dma((3,)), dma((3,)),
                dma((3,)), dma((3,)),
                dma, dma,
                dma((3,)), dma((3,)),
                dma((3,)), dma((3,)),
                dma((3,)), dma((3,)),
                dma((3,)), dma((3,)),
                dma((4,)), dma((4,)),
            ],
            compiler_params=pltpu.CompilerParams(
                collective_id=0, has_side_effects=True, vmem_limit_bytes=40 * 1024 * 1024
            ),
        )(owner, grad, momentum)

    return jax.shard_map(
        body,
        mesh=mesh,
        in_specs=(P("wide", "narrow", None), P("wide", None, "narrow", None), P()),
        out_specs=(P("wide", "narrow", None), P("wide", None, "narrow", None)),
        check_vma=False,
    )
```

time: 260 us -> 59.5 us (0.23)
  waiting for transfers between devices: 199 us -> 0 us
  Pallas kernels: 0 us -> 54.6 us
  starting transfers between devices: 32.5 us -> 0 us
  between operations: 16.3 us -> 0.65 us
  other arithmetic: 5.67 us -> 0 us
  matrix products: 4.25 us -> 0 us
  local copies, waits for them, and re-layouts: 1.33 us -> 4.06 us
    reduce_scatter x1 -> x0, waiting for transfers between devices: 106 us -> none  [orthogonalize(): lax.psum_scatter(lax.dot_general(columns, block, (((0,), (0,)), ((), ()))...]
    all_gather x1 -> x0, waiting for transfers between devices: 84.2 us -> none  [orthogonalize(): piece = lax.all_gather(gram_rows, 'narrow', axis=0, tiled=True)]
    pallas_call x0 -> x1, Pallas kernels: none -> 54.6 us  [body(): pl.pallas_call(functools.partial(kernel, planes), out_shape=(jax.ShapeDty...]
    ppermute x8 -> x0, starting transfers between devices: 32.4 us -> none  [shifted(): return lax.ppermute(value, axis, pairs)]
    ppermute x8 -> x0, waiting for transfers between devices: 8.41 us -> none  [shifted(): return lax.ppermute(value, axis, pairs)]
    dot_general x2 -> x0, matrix products: 4.25 us -> none  [the longest x1 3.5 us: orthogonalize(): lax.dot_general(columns, block, (((0,), (0,)), ((), ())), preferred_eleme...]
    unnamed x4 -> x8, local copies, waits for them, and re-layouts: 0.01 us -> 4.06 us
  transfers between devices with their start and end apart: 10 -> 0, of which waited for: 6 -> 0; matrix products, arithmetic and copies ran while one was open for 1% -> 0% of each run, Pallas kernels for 0% -> 0%
where the time goes in v1:
time: 59.5 us; the launch traced here: 59.3 us
  Pallas kernels  54.6 us (92%)
  local copies, waits for them, and re-layouts  4.06 us (7%)
  between operations  0.65 us (1%)
    pallas_call x1, Pallas kernels, body(): pl.pallas_call(functools.partial(kernel, planes), out_shape=(jax.ShapeDty...  54.6 us
    unnamed x8, local copies, waits for them, and re-layouts  4.06 us

profile of v1, /device:TPU:1, one launch (start us, length us, event | category | flops | bytes accessed | tf_op | source)
XLA Modules:
  0.0 59.3 jit_solution(11717747026163504229)
XLA Ops:
  0.6 0.0 copy-start
  0.6 1.0 %copy-done = bf16[1,2,112,1024]{3,2,1,0:T(8,128)(2,1)S(1)} copy-done((bf16[1,2,112,1024]{3,2,1,0:T(8,128)(2,1)S(1)}, bf16[1,2,112,1024]{3,2,1,0:T(8,128)(2,1)}, u32[]{:S(2)}) %copy-start) | copy-done | bytes 458776
  1.6 0.0 copy-start.1
  1.7 0.9 %copy-done.1 = bf16[1,112,1024]{2,1,0:T(8,128)(2,1)S(1)} copy-done((bf16[1,112,1024]{2,1,0:T(8,128)(2,1)S(1)}, bf16[1,112,1024]{2,1,0:T(8,128)(2,1)}, u32[]{:S(2)}) %copy-start.1) | copy-done | bytes 229400
  2.6 0.0 copy-start.2
  2.6 0.7 %copy-done.2 = s32[32]{0:T(128)S(1)} copy-done((s32[32]{0:T(128)S(1)}, s32[32]{0:T(128)}, u32[]{:S(2)}) %copy-start.2) | copy-done | bytes 152
  3.2 54.6 %shard_map.50 = (bf16[1,112,1024]{2,1,0:T(8,128)(2,1)S(1)}, bf16[1,2,112,1024]{3,2,1,0:T(8,128)(2,1)S(1)}) custom-call(s32[32]{0:T(128)S(1)} %copy-done.2, bf16[1,112,1024]{2,1,0:T(8,128)(2,1)S(1)} %copy-done.1, bf16[1,2,112,1024]{3,2,1,0:T(8,128)(2,1)S(1)} %copy-done), custom_call_target="tpu_custom_call" | custom-call | tf_op jit(solution)/shard_map/pallas_call | solution.py:257
  57.8 0.7 %copy.7 = bf16[1,112,1024]{2,1,0:T(8,128)(2,1)} copy(bf16[1,112,1024]{2,1,0:T(8,128)(2,1)S(1)} %get-tuple-element.4) | data formatting | bytes 458752
  58.5 0.8 %copy.8 = bf16[1,2,112,1024]{3,2,1,0:T(8,128)(2,1)} copy(bf16[1,2,112,1024]{3,2,1,0:T(8,128)(2,1)S(1)} %get-tuple-element.5) | data formatting | bytes 917504
Async XLA Ops:
  0.6 1.0 %copy-start = (bf16[1,2,112,1024]{3,2,1,0:T(8,128)(2,1)S(1)}, bf16[1,2,112,1024]{3,2,1,0:T(8,128)(2,1)}, u32[]{:S(2)}) copy-start(bf16[1,2,112,1024]{3,2,1,0:T(8,128)(2,1)} %mom_ref.1) | copy-start | bytes 1376260
  1.6 0.9 %copy-start.1 = (bf16[1,112,1024]{2,1,0:T(8,128)(2,1)S(1)}, bf16[1,112,1024]{2,1,0:T(8,128)(2,1)}, u32[]{:S(2)}) copy-start(bf16[1,112,1024]{2,1,0:T(8,128)(2,1)} %grad_ref.1) | copy-start | bytes 688132
  2.6 0.7 %copy-start.2 = (s32[32]{0:T(128)S(1)}, s32[32]{0:T(128)}, u32[]{:S(2)}) copy-start(s32[32]{0:T(128)} %owner_ref.1) | copy-start | bytes 388

commit v2 on v1

v2 whole, which is shorter than its diff:
```python
import functools

import jax
import jax.numpy as jnp
from jax import lax
from jax.experimental import pallas as pl
from jax.experimental.pallas import tpu as pltpu
from jax.sharding import PartitionSpec as P

D = 3584
SIDE = 4
TILE = 256
VMEM_LIMIT = 60 * 1024 * 1024

momentum_rate = 0.9
norm_eps = 1e-07

TILES = (
    ((0, 0), (1, 1), (1, 2), (0, 3), (2, 3)),
    ((0, 1), (0, 2), (2, 2), (1, 3), (3, 3)),
)
ROUNDS = len(TILES[0])


def kernel(
    planes,
    owner_hbm,
    grad_ref,
    mom_ref,
    upd_hbm,
    newm_hbm,
    owner_ref,
    upd_ref,
    newm_ref,
    g_own,
    g_nb,
    m_loc,
    m_in,
    xf,
    part,
    r1,
    s1,
    r2,
    gram,
    far_sem,
    local_sem,
    out_sem,
    m_send,
    m_recv,
    g_send,
    g_recv,
    x_send,
    x_recv,
    a_send,
    a_recv,
    b_send,
    b_recv,
    d_send,
    d_recv,
    e_send,
    e_recv,
):
    rows, width = grad_ref.shape[1:]
    columns = width // TILE
    strip = TILE // SIDE
    w = lax.axis_index("wide")
    n = lax.axis_index("narrow")
    z, c = w // 2, w % 2
    y, x = n // SIDE, n % SIDE
    up, down = (z + 1) % planes, (z + planes - 1) % planes
    sibling = (z * 2 + 1 - c, n)
    near = jnp.where(c == 0, down, up)

    first = jnp.where(c == 0, x, y)
    second = jnp.where(c == 0, y, x)

    def first_peer(k):
        there = (first + k) % SIDE
        return (w, jnp.where(c == 0, y * SIDE + there, there * SIDE + x))

    def second_peer(k):
        there = (second + k) % SIDE
        return (w, jnp.where(c == 0, there * SIDE + x, y * SIDE + there))

    def remote(src, dst, send, recv, device):
        return pltpu.make_async_remote_copy(
            src_ref=src,
            dst_ref=dst,
            send_sem=send,
            recv_sem=recv,
            device_id=device,
            device_id_type=pl.DeviceIdType.MESH,
        )

    sent = []

    def push(*args):
        copy = remote(*args)
        copy.start()
        sent.append(copy)

    def arrived(ref, recv):
        remote(ref, ref, recv, recv, sibling).wait_recv()

    load_m = pltpu.make_async_copy(mom_ref.at[0], m_loc, local_sem.at[0])
    load_g = pltpu.make_async_copy(grad_ref.at[0], g_own.at[c], local_sem.at[1])
    load_o = pltpu.make_async_copy(owner_hbm, owner_ref, local_sem.at[2])
    load_o.start()
    load_m.start()
    load_g.start()

    barrier = pltpu.get_barrier_semaphore()
    partners = [sibling, (near * 2, n), (near * 2 + 1, n), (jnp.where(c == 0, up, down) * 2 + c, n)]
    for k in (1, 3):
        partners += [first_peer(k), second_peer(k)]
    for device in partners:
        pl.semaphore_signal(barrier, inc=1, device_id=device, device_id_type=pl.DeviceIdType.MESH)
    pl.semaphore_wait(barrier, len(partners))
    pl.semaphore_signal(far_sem.at[0], inc=1, device_id=first_peer(3), device_id_type=pl.DeviceIdType.MESH)
    pl.semaphore_signal(far_sem.at[1], inc=1, device_id=second_peer(3), device_id_type=pl.DeviceIdType.MESH)

    slot = jnp.where(c == 0, 2, 1)

    def lanes(j):
        return slice(j * TILE, (j + 1) * TILE)

    for j in range(columns):
        push(mom_ref.at[0, 0, :, lanes(j)], m_in.at[j, slot], m_send.at[1, j], m_recv.at[j, slot], (near * 2, n))
        push(mom_ref.at[0, 1, :, lanes(j)], m_in.at[j, slot], m_send.at[2, j], m_recv.at[j, slot], (near * 2 + 1, n))
        push(mom_ref.at[0, 1 - c, :, lanes(j)], m_in.at[j, 0], m_send.at[0, j], m_recv.at[j, 0], sibling)
    load_o.wait()
    load_m.wait()
    load_g.wait()

    offset = (owner_ref[z] - 2 * z + 2 * planes) % (2 * planes)
    mine = pl.ds(pl.multiple_of(c * rows, 16), rows)
    other = pl.ds(pl.multiple_of((1 - c) * rows, 16), rows)

    def make_x(j):
        for k in range(3):
            arrived(m_in.at[j, k], m_recv.at[j, k])
        stored = jnp.where(
            offset == c,
            m_loc[c, :, lanes(j)],
            jnp.where(offset == 1 - c, m_in[j, 0], jnp.where(offset == 2, m_in[j, 2], m_in[j, 1])),
        )
        grad_value = g_own[c, :, lanes(j)].astype(jnp.float32)
        velocity = momentum_rate * stored.astype(jnp.float32) + grad_value
        xf[j, mine, :] = (grad_value + momentum_rate * velocity).astype(jnp.bfloat16)
        push(xf.at[j, mine], xf.at[j, mine], x_send.at[j], x_recv.at[j], sibling)
        arrived(xf.at[j, other], x_recv.at[j])

    def strip_of(k):
        return pl.ds(pl.multiple_of(k * strip, 16), strip)

    def make_tile(r):
        i = jnp.where(c == 0, TILES[0][r][0], TILES[1][r][0])
        j = jnp.where(c == 0, TILES[0][r][1], TILES[1][r][1])
        tile = lax.dot_general(xf[i], xf[j], (((0,), (0,)), ((), ())), preferred_element_type=jnp.float32)
        part[r] = tile.astype(jnp.bfloat16)
        for k in (2, 1, 3):
            there = (first + k) % SIDE
            push(part.at[r, strip_of(there)], r1.at[r, k - 1], a_send.at[r, k - 1], a_recv.at[r, k - 1], first_peer(k))

    def sum_first(r):
        acc = part[r, strip_of(first), :].astype(jnp.float32)
        for k in range(3):
            arrived(r1.at[r, k], a_recv.at[r, k])
        for k in range(3):
            acc = acc + r1[r, k].astype(jnp.float32)
        s1[r] = acc.astype(jnp.bfloat16)
        for k in (2, 1, 3):
            push(s1.at[r], r2.at[r, k - 1], b_send.at[r, k - 1], b_recv.at[r, k - 1], second_peer(k))

    def sum_second(r):
        acc = s1[r].astype(jnp.float32)
        for k in range(3):
            arrived(r2.at[r, k], b_recv.at[r, k])
        for k in range(3):
            acc = acc + r2[r, k].astype(jnp.float32)
        own = strip_of(first)
        gram[c, r, own, :] = acc.astype(jnp.bfloat16)
        for k in (2, 1, 3):
            push(gram.at[c, r, own], gram.at[c, r, own], d_send.at[r, k - 1], d_recv.at[r, k - 1], first_peer(k))

    def pass_tile(r):
        for k in range(1, SIDE):
            there = strip_of((first + SIDE - k) % SIDE)
            arrived(gram.at[c, r, there], d_recv.at[r, k - 1])
        push(gram.at[c, r], gram.at[c, r], e_send.at[r], e_recv.at[r], sibling)

    stored_out = []

    def store(src, dst, sem):
        copy = pltpu.make_async_copy(src, dst, sem)
        copy.start()
        stored_out.append(copy)

    def new_momentum(h):
        live_main = owner_ref[z] == w
        live_near = owner_ref[near] == w
        kept = jnp.where(live_main, g_own[h], g_nb[h]).astype(jnp.float32)
        state = momentum_rate * m_loc[h].astype(jnp.float32) + kept
        newm_ref[h] = jnp.where(jnp.logical_or(live_main, live_near), state, 0.0).astype(jnp.bfloat16)
        store(newm_ref.at[h], newm_hbm.at[0, h], out_sem.at[h])

    make_x(0)
    make_x(1)
    pl.semaphore_wait(far_sem.at[0], 1)
    pl.semaphore_wait(far_sem.at[1], 1)
    make_tile(0)
    make_x(2)
    make_tile(1)
    make_tile(2)
    make_x(3)
    make_tile(3)
    make_tile(4)

    push(grad_ref.at[0], g_nb.at[c], g_send.at[1], g_recv.at[1 + c], (up * 2, n))
    push(grad_ref.at[0], g_nb.at[c], g_send.at[2], g_recv.at[1 + c], (down * 2 + 1, n))
    push(grad_ref.at[0], g_own.at[c], g_send.at[0], g_recv.at[0], sibling)

    sum_first(0)
    sum_first(1)
    sum_first(2)
    sum_first(3)
    sum_second(0)
    sum_first(4)
    sum_second(1)
    sum_second(2)
    sum_second(3)
    pass_tile(0)
    sum_second(4)
    pass_tile(1)
    arrived(g_own.at[1 - c], g_recv.at[0])
    for h in range(2):
        arrived(g_nb.at[h], g_recv.at[1 + h])
        new_momentum(h)
    pass_tile(2)
    pass_tile(3)
    pass_tile(4)
    for r in range(ROUNDS):
        arrived(gram.at[1 - c, r], e_recv.at[r])

    row_ids = lax.broadcasted_iota(jnp.int32, (TILE, TILE), 0)
    col_ids = lax.broadcasted_iota(jnp.int32, (TILE, TILE), 1)
    diagonal = jnp.zeros((TILE, TILE), jnp.float32)
    place = {}
    for core in range(2):
        for r, pair in enumerate(TILES[core]):
            place[pair] = (core, r)
            if pair[0] == pair[1]:
                diagonal = diagonal + jnp.where(row_ids == col_ids, gram[core, r].astype(jnp.float32), 0.0)
    trace_sum = jnp.sum(jnp.sum(diagonal, axis=0, keepdims=True), axis=1, keepdims=True)
    factor = jnp.sqrt(jnp.float32(width)) / (jnp.sqrt(trace_sum) + norm_eps)
    for j in range(columns):
        product = jnp.zeros((rows, TILE), jnp.float32)
        for i in range(columns):
            core, r = place[(min(i, j), max(i, j))]
            dims = (((1,), (0,)), ((), ())) if i <= j else (((1,), (1,)), ((), ()))
            product = product + lax.dot_general(
                xf[i, mine, :], gram[core, r], dims, preferred_element_type=jnp.float32
            )
        block = xf[j, mine, :].astype(jnp.float32)
        result = factor * (1.5 * block - 0.5 * factor * factor * product)
        upd_ref[j] = (result * jnp.sqrt(jnp.float32(D))).astype(jnp.bfloat16)
        store(upd_ref.at[j], upd_hbm.at[0, :, lanes(j)], out_sem.at[2 + j])

    for copy in sent:
        copy.wait_send()
    for copy in stored_out:
        copy.wait()


def finish(upd_in, newm_in, upd_out, newm_out, upd, newm, load_sem, store_sem):
    halves = newm.shape[0]
    pieces = [(newm_in.at[0, h], newm.at[h], newm_out.at[0, h]) for h in range(halves)]
    pieces.append((upd_in.at[0], upd, upd_out.at[0]))
    loads = [pltpu.make_async_copy(src, held, load_sem.at[i]) for i, (src, held, dst) in enumerate(pieces)]
    stores = [pltpu.make_async_copy(held, dst, store_sem.at[i]) for i, (src, held, dst) in enumerate(pieces)]
    for copy in loads:
        copy.start()
    for load, copy in zip(loads, stores):
        load.wait()
        copy.start()
    for copy in stores:
        copy.wait()


def solution(mesh):
    planes = mesh.shape["wide"] // 2

    def body(grad, momentum, owner):
        rows, width = grad.shape[1:]
        columns = width // TILE
        strip = TILE // SIDE
        kind = jnp.bfloat16
        dma = pltpu.SemaphoreType.DMA
        results = pl.pallas_call(
            functools.partial(kernel, planes),
            out_shape=(
                jax.ShapeDtypeStruct(grad.shape, kind),
                jax.ShapeDtypeStruct(momentum.shape, kind),
            ),
            in_specs=[
                pl.BlockSpec(memory_space=pl.ANY),
                pl.BlockSpec(memory_space=pl.ANY),
                pl.BlockSpec(memory_space=pl.ANY),
            ],
            out_specs=(
                pl.BlockSpec(memory_space=pl.ANY),
                pl.BlockSpec(memory_space=pl.ANY),
            ),
            scratch_shapes=[
                pltpu.SMEM(owner.shape, owner.dtype),
                pltpu.VMEM((columns, rows, TILE), kind),
                pltpu.VMEM((2, rows, width), kind),
                pltpu.VMEM((2, rows, width), kind),
                pltpu.VMEM((2, rows, width), kind),
                pltpu.VMEM((2, rows, width), kind),
                pltpu.VMEM((columns, 3, rows, TILE), kind),
                pltpu.VMEM((columns, 2 * rows, TILE), kind),
                pltpu.VMEM((ROUNDS, TILE, TILE), kind),
                pltpu.VMEM((ROUNDS, 3, strip, TILE), kind),
                pltpu.VMEM((ROUNDS, strip, TILE), kind),
                pltpu.VMEM((ROUNDS, 3, strip, TILE), kind),
                pltpu.VMEM((2, ROUNDS, TILE, TILE), kind),
                pltpu.SemaphoreType.REGULAR((2,)),
                dma((3,)),
                dma((2 + columns,)),
                dma((3, columns)),
                dma((columns, 3)),
                dma((3,)),
                dma((3,)),
                dma((columns,)),
                dma((columns,)),
                dma((ROUNDS, 3)),
                dma((ROUNDS, 3)),
                dma((ROUNDS, 3)),
                dma((ROUNDS, 3)),
                dma((ROUNDS, 3)),
                dma((ROUNDS, 3)),
                dma((ROUNDS,)),
                dma((ROUNDS,)),
            ],
            compiler_params=pltpu.CompilerParams(
                collective_id=0, has_side_effects=True, vmem_limit_bytes=VMEM_LIMIT
            ),
        )(owner, grad, momentum)
        return pl.pallas_call(
            finish,
            out_shape=(
                jax.ShapeDtypeStruct(grad.shape, kind),
                jax.ShapeDtypeStruct(momentum.shape, kind),
            ),
            in_specs=[pl.BlockSpec(memory_space=pl.ANY)] * 2,
            out_specs=(pl.BlockSpec(memory_space=pl.ANY),) * 2,
            scratch_shapes=[
                pltpu.VMEM((rows, width), kind),
                pltpu.VMEM((2, rows, width), kind),
                dma((3,)),
                dma((3,)),
            ],
            compiler_params=pltpu.CompilerParams(vmem_limit_bytes=VMEM_LIMIT),
        )(*results)

    return jax.shard_map(
        body,
        mesh=mesh,
        in_specs=(P("wide", "narrow", None), P("wide", None, "narrow", None), P()),
        out_specs=(P("wide", "narrow", None), P("wide", None, "narrow", None)),
        check_vma=False,
    )
```

time: 59.5 us -> 50.2 us (0.84)
  Pallas kernels: 54.6 us -> 49.4 us
  local copies, waits for them, and re-layouts: 4.06 us -> 0 us
    pallas_call x1, Pallas kernels: 54.6 us -> 47.5 us  [body(): pl.pallas_call(functools.partial(kernel, planes), out_shape=(jax.ShapeDty...]
    unnamed x8 -> x0, local copies, waits for them, and re-layouts: 4.06 us -> none
    pallas_call x0 -> x1, Pallas kernels: none -> 1.9 us  [body(): pl.pallas_call(finish, out_shape=(jax.ShapeDtypeStruct(grad.shape, kind),...]
where the time goes in v2:
time: 50.2 us; the launch traced here: 50 us
  Pallas kernels  49.4 us (98%)
  between operations  0.64 us (1%)
    pallas_call x1, Pallas kernels, body(): pl.pallas_call(functools.partial(kernel, planes), out_shape=(jax.ShapeDty...  47.5 us
    pallas_call x1, Pallas kernels, body(): pl.pallas_call(finish, out_shape=(jax.ShapeDtypeStruct(grad.shape, kind),...  1.9 us

profile of v2, /device:TPU:1, one launch (start us, length us, event | category | flops | bytes accessed | tf_op | source)
XLA Modules:
  0.0 50.0 jit_solution(4199034314299065711)
XLA Ops:
  0.6 47.5 %shard_map.50 = (bf16[1,112,1024]{2,1,0:T(8,128)(2,1)}, bf16[1,2,112,1024]{3,2,1,0:T(8,128)(2,1)}) custom-call(s32[32]{0:T(128)} %owner_hbm.1, bf16[1,112,1024]{2,1,0:T(8,128)(2,1)} %grad_ref.1, bf16[1,2,112,1024]{3,2,1,0:T(8,128)(2,1)} %mom_ref.1), custom_call_target="tpu_custom_call" | custom-call | tf_op jit(solution)/shard_map/pallas_call | solution.py:299
  48.1 1.9 %shard_map.51 = (bf16[1,112,1024]{2,1,0:T(8,128)(2,1)}, bf16[1,2,112,1024]{3,2,1,0:T(8,128)(2,1)}) custom-call(bf16[1,112,1024]{2,1,0:T(8,128)(2,1)} %get-tuple-element.4.upd_in, bf16[1,2,112,1024]{3,2,1,0:T(8,128)(2,1)} %get-tuple-element.5.newm_in), custom_call_target="tpu_custom_call" | custom-call | tf_op jit(solution)/shard_map/pallas_call | solution.py:350

commit v3 on v2

--- a/solution.py
+++ b/solution.py
@@ -42,6 +42,7 @@
     s1,
     r2,
     gram,
+    near_sem,
     far_sem,
     local_sem,
     out_sem,
@@ -109,15 +110,26 @@
     load_m.start()
     load_g.start()
 
+    def signal(sem, device):
+        pl.semaphore_signal(sem, inc=1, device_id=device, device_id_type=pl.DeviceIdType.MESH)
+
     barrier = pltpu.get_barrier_semaphore()
-    partners = [sibling, (near * 2, n), (near * 2 + 1, n), (jnp.where(c == 0, up, down) * 2 + c, n)]
+    signal(barrier, (jnp.where(c == 0, down * 2, up * 2), n))
+    signal(barrier, (down * 2 + 1, n))
+    signal(barrier, sibling)
     for k in (1, 3):
-        partners += [first_peer(k), second_peer(k)]
-    for device in partners:
-        pl.semaphore_signal(barrier, inc=1, device_id=device, device_id_type=pl.DeviceIdType.MESH)
-    pl.semaphore_wait(barrier, len(partners))
-    pl.semaphore_signal(far_sem.at[0], inc=1, device_id=first_peer(3), device_id_type=pl.DeviceIdType.MESH)
-    pl.semaphore_signal(far_sem.at[1], inc=1, device_id=second_peer(3), device_id_type=pl.DeviceIdType.MESH)
+        signal(barrier, (z * 2, y * SIDE + (x + k) % SIDE))
+        signal(barrier, (z * 2, (y + k) % SIDE * SIDE + x))
+
+    @pl.when(c == 0)
+    def _():
+        signal(barrier, (up * 2, n))
+
+    pl.semaphore_wait(barrier, jnp.where(c == 0, 12, 3))
+
+    @pl.when(c == 0)
+    def _():
+        signal(near_sem, sibling)
 
     slot = jnp.where(c == 0, 2, 1)
 
@@ -132,9 +144,21 @@
     load_m.wait()
     load_g.wait()
 
+    @pl.when(c == 1)
+    def _():
+        pl.semaphore_wait(near_sem, 1)
+
+    signal(far_sem.at[0], first_peer(3))
+    signal(far_sem.at[1], second_peer(3))
+
     offset = (owner_ref[z] - 2 * z + 2 * planes) % (2 * planes)
     mine = pl.ds(pl.multiple_of(c * rows, 16), rows)
     other = pl.ds(pl.multiple_of((1 - c) * rows, 16), rows)
+
+    def send_gradient():
+        push(grad_ref.at[0], g_nb.at[c], g_send.at[1], g_recv.at[1 + c], (up * 2, n))
+        push(grad_ref.at[0], g_nb.at[c], g_send.at[2], g_recv.at[1 + c], (down * 2 + 1, n))
+        push(grad_ref.at[0], g_own.at[c], g_send.at[0], g_recv.at[0], sibling)
 
     def make_x(j):
         for k in range(3):
@@ -148,6 +172,8 @@
         velocity = momentum_rate * stored.astype(jnp.float32) + grad_value
         xf[j, mine, :] = (grad_value + momentum_rate * velocity).astype(jnp.bfloat16)
         push(xf.at[j, mine], xf.at[j, mine], x_send.at[j], x_recv.at[j], sibling)
+        if j == columns - 1:
+            send_gradient()
         arrived(xf.at[j, other], x_recv.at[j])
 
     def strip_of(k):
@@ -215,10 +241,6 @@
     make_x(3)
     make_tile(3)
     make_tile(4)
-
-    push(grad_ref.at[0], g_nb.at[c], g_send.at[1], g_recv.at[1 + c], (up * 2, n))
-    push(grad_ref.at[0], g_nb.at[c], g_send.at[2], g_recv.at[1 + c], (down * 2 + 1, n))
-    push(grad_ref.at[0], g_own.at[c], g_send.at[0], g_recv.at[0], sibling)
 
     sum_first(0)
     sum_first(1)
@@ -232,37 +254,50 @@
     pass_tile(0)
     sum_second(4)
     pass_tile(1)
+    pass_tile(2)
+    pass_tile(3)
+
+    for copy in sent[:-2 * SIDE]:
+        copy.wait_send()
+    del sent[:-2 * SIDE]
+
+    row_ids = lax.broadcasted_iota(jnp.int32, (TILE, TILE), 0)
+    col_ids = lax.broadcasted_iota(jnp.int32, (TILE, TILE), 1)
+    block = [xf[j, mine, :] for j in range(columns)]
+    product = [jnp.zeros((rows, TILE), jnp.float32) for j in range(columns)]
+    diagonal = [jnp.zeros((TILE, TILE), jnp.float32)]
+
+    def multiply(core, r):
+        i, j = TILES[core][r]
+        tile = gram[core, r]
+        product[j] = product[j] + lax.dot_general(
+            block[i], tile, (((1,), (0,)), ((), ())), preferred_element_type=jnp.float32
+        )
+        if i == j:
+            diagonal[0] = diagonal[0] + jnp.where(row_ids == col_ids, tile.astype(jnp.float32), 0.0)
+        else:
+            product[i] = product[i] + lax.dot_general(
+                block[j], tile, (((1,), (1,)), ((), ())), preferred_element_type=jnp.float32
+            )
+
+    for r in range(ROUNDS - 2):
+        arrived(gram.at[1 - c, r], e_recv.at[r])
+        multiply(0, r)
+        multiply(1, r)
+    pass_tile(ROUNDS - 1)
     arrived(g_own.at[1 - c], g_recv.at[0])
     for h in range(2):
         arrived(g_nb.at[h], g_recv.at[1 + h])
         new_momentum(h)
-    pass_tile(2)
-    pass_tile(3)
-    pass_tile(4)
-    for r in range(ROUNDS):
+    for r in range(ROUNDS - 2, ROUNDS):
         arrived(gram.at[1 - c, r], e_recv.at[r])
-
-    row_ids = lax.broadcasted_iota(jnp.int32, (TILE, TILE), 0)
-    col_ids = lax.broadcasted_iota(jnp.int32, (TILE, TILE), 1)
-    diagonal = jnp.zeros((TILE, TILE), jnp.float32)
-    place = {}
-    for core in range(2):
-        for r, pair in enumerate(TILES[core]):
-            place[pair] = (core, r)
-            if pair[0] == pair[1]:
-                diagonal = diagonal + jnp.where(row_ids == col_ids, gram[core, r].astype(jnp.float32), 0.0)
-    trace_sum = jnp.sum(jnp.sum(diagonal, axis=0, keepdims=True), axis=1, keepdims=True)
+        multiply(0, r)
+        multiply(1, r)
+
+    trace_sum = jnp.sum(jnp.sum(diagonal[0], axis=0, keepdims=True), axis=1, keepdims=True)
     factor = jnp.sqrt(jnp.float32(width)) / (jnp.sqrt(trace_sum) + norm_eps)
     for j in range(columns):
-        product = jnp.zeros((rows, TILE), jnp.float32)
-        for i in range(columns):
-            core, r = place[(min(i, j), max(i, j))]
-            dims = (((1,), (0,)), ((), ())) if i <= j else (((1,), (1,)), ((), ()))
-            product = product + lax.dot_general(
-                xf[i, mine, :], gram[core, r], dims, preferred_element_type=jnp.float32
-            )
-        block = xf[j, mine, :].astype(jnp.float32)
-        result = factor * (1.5 * block - 0.5 * factor * factor * product)
+        result = factor * (1.5 * block[j].astype(jnp.float32) - 0.5 * factor * factor * product[j])
         upd_ref[j] = (result * jnp.sqrt(jnp.float32(D))).astype(jnp.bfloat16)
         store(upd_ref.at[j], upd_hbm.at[0, :, lanes(j)], out_sem.at[2 + j])
 
@@ -325,6 +360,7 @@
                 pltpu.VMEM((ROUNDS, strip, TILE), kind),
                 pltpu.VMEM((ROUNDS, 3, strip, TILE), kind),
                 pltpu.VMEM((2, ROUNDS, TILE, TILE), kind),
+                pltpu.SemaphoreType.REGULAR,
                 pltpu.SemaphoreType.REGULAR((2,)),
                 dma((3,)),
                 dma((2 + columns,)),

time: 50.2 us -> 48.9 us (0.974)
  Pallas kernels: 49.4 us -> 48.1 us
    pallas_call x1, Pallas kernels: 47.5 us -> 46.2 us  [body(): pl.pallas_call(functools.partial(kernel, planes), out_shape=(jax.ShapeDty...]
where the time goes in v3:
time: 48.9 us; the launch traced here: 48.7 us
  Pallas kernels  48.1 us (98%)
  between operations  0.64 us (1%)
    pallas_call x1, Pallas kernels, body(): pl.pallas_call(functools.partial(kernel, planes), out_shape=(jax.ShapeDty...  46.2 us
    pallas_call x1, Pallas kernels, body(): pl.pallas_call(finish, out_shape=(jax.ShapeDtypeStruct(grad.shape, kind),...  1.9 us

profile of v3, /device:TPU:1, one launch (start us, length us, event | category | flops | bytes accessed | tf_op | source)
XLA Modules:
  0.0 48.7 jit_solution(14642957286374248890)
XLA Ops:
  0.6 46.2 %shard_map.50 = (bf16[1,112,1024]{2,1,0:T(8,128)(2,1)}, bf16[1,2,112,1024]{3,2,1,0:T(8,128)(2,1)}) custom-call(s32[32]{0:T(128)} %owner_hbm.1, bf16[1,112,1024]{2,1,0:T(8,128)(2,1)} %grad_ref.1, bf16[1,2,112,1024]{3,2,1,0:T(8,128)(2,1)} %mom_ref.1), custom_call_target="tpu_custom_call" | custom-call | tf_op jit(solution)/shard_map/pallas_call | solution.py:334
  46.8 1.9 %shard_map.51 = (bf16[1,112,1024]{2,1,0:T(8,128)(2,1)}, bf16[1,2,112,1024]{3,2,1,0:T(8,128)(2,1)}) custom-call(bf16[1,112,1024]{2,1,0:T(8,128)(2,1)} %get-tuple-element.4.upd_in, bf16[1,2,112,1024]{3,2,1,0:T(8,128)(2,1)} %get-tuple-element.5.newm_in), custom_call_target="tpu_custom_call" | custom-call | tf_op jit(solution)/shard_map/pallas_call | solution.py:386

commit v4 on v3

--- a/solution.py
+++ b/solution.py
@@ -60,6 +60,8 @@
     d_recv,
     e_send,
     e_recv,
+    h_send,
+    h_recv,
 ):
     rows, width = grad_ref.shape[1:]
     columns = width // TILE
@@ -209,6 +211,13 @@
         for k in (2, 1, 3):
             push(gram.at[c, r, own], gram.at[c, r, own], d_send.at[r, k - 1], d_recv.at[r, k - 1], first_peer(k))
 
+    def pass_strips(r):
+        for k in (0, 1, 3, 2):
+            there = strip_of((first + SIDE - k) % SIDE)
+            if k:
+                arrived(gram.at[c, r, there], d_recv.at[r, k - 1])
+            push(gram.at[c, r, there], gram.at[c, r, there], h_send.at[k], h_recv.at[k], sibling)
+
     def pass_tile(r):
         for k in range(1, SIDE):
             there = strip_of((first + SIDE - k) % SIDE)
@@ -242,17 +251,11 @@
     make_tile(3)
     make_tile(4)
 
-    sum_first(0)
-    sum_first(1)
-    sum_first(2)
-    sum_first(3)
-    sum_second(0)
-    sum_first(4)
-    sum_second(1)
-    sum_second(2)
-    sum_second(3)
+    for r in range(ROUNDS):
+        sum_first(r)
+    for r in range(ROUNDS):
+        sum_second(r)
     pass_tile(0)
-    sum_second(4)
     pass_tile(1)
     pass_tile(2)
     pass_tile(3)
@@ -284,15 +287,19 @@
         arrived(gram.at[1 - c, r], e_recv.at[r])
         multiply(0, r)
         multiply(1, r)
-    pass_tile(ROUNDS - 1)
+    pass_strips(ROUNDS - 1)
     arrived(g_own.at[1 - c], g_recv.at[0])
     for h in range(2):
         arrived(g_nb.at[h], g_recv.at[1 + h])
         new_momentum(h)
-    for r in range(ROUNDS - 2, ROUNDS):
-        arrived(gram.at[1 - c, r], e_recv.at[r])
-        multiply(0, r)
-        multiply(1, r)
+    arrived(gram.at[1 - c, ROUNDS - 2], e_recv.at[ROUNDS - 2])
+    multiply(0, ROUNDS - 2)
+    multiply(1, ROUNDS - 2)
+    for k in range(SIDE):
+        there = strip_of((second + SIDE - k) % SIDE)
+        arrived(gram.at[1 - c, ROUNDS - 1, there], h_recv.at[k])
+    multiply(0, ROUNDS - 1)
+    multiply(1, ROUNDS - 1)
 
     trace_sum = jnp.sum(jnp.sum(diagonal[0], axis=0, keepdims=True), axis=1, keepdims=True)
     factor = jnp.sqrt(jnp.float32(width)) / (jnp.sqrt(trace_sum) + norm_eps)
@@ -378,6 +385,8 @@
                 dma((ROUNDS, 3)),
                 dma((ROUNDS,)),
                 dma((ROUNDS,)),
+                dma((SIDE,)),
+                dma((SIDE,)),
             ],
             compiler_params=pltpu.CompilerParams(
                 collective_id=0, has_side_effects=True, vmem_limit_bytes=VMEM_LIMIT

time: 48.9 us -> 48.8 us (level)
  no operation moved by 1% of the time
where the time goes in v4:
time: 48.8 us; the launch traced here: 48.6 us
  Pallas kernels  48 us (98%)
  between operations  0.64 us (1%)
    pallas_call x1, Pallas kernels, body(): pl.pallas_call(functools.partial(kernel, planes), out_shape=(jax.ShapeDty...  46.1 us
    pallas_call x1, Pallas kernels, body(): pl.pallas_call(finish, out_shape=(jax.ShapeDtypeStruct(grad.shape, kind),...  1.9 us

profile of v4, /device:TPU:1, one launch (start us, length us, event | category | flops | bytes accessed | tf_op | source)
XLA Modules:
  0.0 48.6 jit_solution(11171204815176167993)
XLA Ops:
  0.6 46.1 %shard_map.50 = (bf16[1,112,1024]{2,1,0:T(8,128)(2,1)}, bf16[1,2,112,1024]{3,2,1,0:T(8,128)(2,1)}) custom-call(s32[32]{0:T(128)} %owner_hbm.1, bf16[1,112,1024]{2,1,0:T(8,128)(2,1)} %grad_ref.1, bf16[1,2,112,1024]{3,2,1,0:T(8,128)(2,1)} %mom_ref.1), custom_call_target="tpu_custom_call" | custom-call | tf_op jit(solution)/shard_map/pallas_call | solution.py:341
  46.7 1.9 %shard_map.51 = (bf16[1,112,1024]{2,1,0:T(8,128)(2,1)}, bf16[1,2,112,1024]{3,2,1,0:T(8,128)(2,1)}) custom-call(bf16[1,112,1024]{2,1,0:T(8,128)(2,1)} %get-tuple-element.4.upd_in, bf16[1,2,112,1024]{3,2,1,0:T(8,128)(2,1)} %get-tuple-element.5.newm_in), custom_call_target="tpu_custom_call" | custom-call | tf_op jit(solution)/shard_map/pallas_call | solution.py:395
